TPU v7x, 768 devices: a whole 4x8x12 slice. The times are simulated.
768 devices in a mesh: dom: 192 (over y, z, core), help: 4 (over x).
Axes of the slice: x: 4, y: 8, z: 12, core: 2. Of those that a mesh axis runs over, the one named last changes fastest.
Arguments:
- features: bfloat16 [196608, 256], P(('dom', 'help')), may hold values from -6 to 6
- tile_vals: bfloat16 [36864, 128, 128], P(('dom', 'help')), as said below
- tile_dst: int32 [36864], P(('dom', 'help')), may hold values from 0 to 7
- tile_src: int32 [36864], P(('dom', 'help')), may hold values from 0 to 39
- w_self: bfloat16 [256, 256], replicated, may hold values from -0.375 to 0.375
- w_neigh: bfloat16 [256, 256], replicated, may hold values from -0.375 to 0.375
- cotangent: bfloat16 [196608, 256], P(('dom', 'help')), may hold values from -6 to 6
Outputs:
- hidden_out: bfloat16 [196608, 256], P(('dom', 'help'))
- grad_features: float32 [196608, 256], P(('dom', 'help'))
- grad_self: float32 [256, 256], replicated
- grad_neigh: float32 [256, 256], replicated
Inputs may be any that keep to these rules, and one draw needn't show every extreme that they name: `tile_vals`: edge weights are non-negative.
All inputs are finite; a program needn't handle non-finite values.
Results may differ from a plain program's by a relative error of at most 0.013.
Values may be sent and summed in bfloat16 or wider, within the bound.
A program may use at most 64 MiB of HBM per device.

v0:
```python
import jax
import jax.numpy as jnp
from jax import lax
from jax.sharding import PartitionSpec as P

RADIUS = 2


def shifted_2(block, axis, distance):
    devices = range(lax.axis_size(axis))
    route = [((i - distance) % len(devices), i) for i in devices]
    return lax.ppermute(block, axis, route)


def on_device(features, tile_vals, tile_dst, tile_src, w_self, w_neigh, cotangent):
    helpers = lax.axis_size("help")
    row_count, feat_width = features.shape
    blk_rows = tile_vals.shape[1]
    part_blocks = helpers * row_count // blk_rows
    band_span = 2 * RADIUS + 1
    band_blocks = band_span * part_blocks
    shifted = []
    for offset in range(-RADIUS, RADIUS + 1):
        if offset == 0:
            shifted.append(features)
        else:
            shifted.append(shifted_2(features, "dom", -offset))
    band_local = jnp.stack(shifted)
    gathered = lax.all_gather(band_local, "help", axis=1, tiled=True)
    source_rows = gathered.reshape(band_blocks, blk_rows, feat_width)
    picked = source_rows[tile_src]
    products = jnp.einsum("tij,tjf->tif", tile_vals, picked, preferred_element_type=jnp.float32)
    dest_onehot = (tile_dst[None, :] == jnp.arange(part_blocks, dtype=jnp.int32)[:, None]).astype(
        jnp.float32
    )
    partial_agg = jnp.einsum("dt,tif->dif", dest_onehot, products, precision=lax.Precision.HIGHEST)
    partial_agg = partial_agg.reshape(part_blocks * blk_rows, feat_width)
    aggregate = lax.psum_scatter(partial_agg, "help", scatter_dimension=0, tiled=True).astype(
        jnp.bfloat16
    )
    pre_act = jnp.dot(features, w_self, preferred_element_type=jnp.float32) + jnp.dot(
        aggregate, w_neigh, preferred_element_type=jnp.float32
    )
    squash = jax.nn.sigmoid(pre_act)
    hidden_out = (pre_act * squash).astype(jnp.bfloat16)
    slope = squash * (1.0 + pre_act * (1.0 - squash))
    grad_pre = (cotangent.astype(jnp.float32) * slope).astype(jnp.bfloat16)
    self_term = jnp.einsum("rf,rg->fg", features, grad_pre, preferred_element_type=jnp.float32)
    neigh_term = jnp.einsum("rf,rg->fg", aggregate, grad_pre, preferred_element_type=jnp.float32)
    grad_self, grad_neigh = lax.psum((self_term, neigh_term), ("dom", "help"))
    dest_grad = jnp.einsum(
        "rg,fg->rf", grad_pre, w_neigh, preferred_element_type=jnp.float32
    ).astype(jnp.bfloat16)
    dest_part = lax.all_gather(dest_grad, "help", axis=0, tiled=True).reshape(
        part_blocks, blk_rows, feat_width
    )
    dest_rows = dest_part[tile_dst]
    back_tiles = jnp.einsum(
        "tji,tjf->tif", tile_vals, dest_rows, preferred_element_type=jnp.float32
    )
    source_onehot = (tile_src[None, :] == jnp.arange(band_blocks, dtype=jnp.int32)[:, None]).astype(
        jnp.float32
    )
    band_terms = jnp.einsum(
        "st,tif->sif", source_onehot, back_tiles, precision=lax.Precision.HIGHEST
    )
    band_terms = band_terms.reshape(band_span, part_blocks * blk_rows, feat_width)
    own_term = jnp.einsum("rg,fg->rf", grad_pre, w_self, preferred_element_type=jnp.float32)
    arrived = band_terms[RADIUS]
    for offset in range(-RADIUS, RADIUS + 1):
        if offset != 0:
            arrived = arrived + shifted_2(
                band_terms[offset + RADIUS].astype(jnp.bfloat16), "dom", offset
            ).astype(jnp.float32)
    returned = lax.psum_scatter(
        arrived.astype(jnp.bfloat16), "help", scatter_dimension=0, tiled=True
    ).astype(jnp.float32)
    grad_features = own_term + returned
    return (hidden_out, grad_features, grad_self, grad_neigh)


def solution(mesh):
    in_specs = (
        P(("dom", "help"), None),
        P(("dom", "help"), None, None),
        P(("dom", "help")),
        P(("dom", "help")),
        P(),
        P(),
        P(("dom", "help"), None),
    )
    out_specs = (P(("dom", "help"), None), P(("dom", "help"), None), P(), P())
    return jax.shard_map(
        on_device, mesh=mesh, in_specs=in_specs, out_specs=out_specs, check_vma=False
    )
```

profile of v0, /device:TPU:1, one launch (start us, length us, event | category | flops | bytes accessed | tf_op | source)
XLA Modules:
  0.0 689.4 jit_solution(10949591171726869952)
XLA Ops:
  7.2 5.0 collective-permute-start
  12.2 4.8 collective-permute-start.1
  17.0 6.6 collective-permute-start.2
  23.7 8.2 %collective-permute-start.3 = (bf16[256,256]{1,0:T(8,128)(2,1)}, bf16[256,256]{1,0:T(8,128)(2,1)S(1)}, u32[]{:S(2)}, u32[]{:S(2)}) collective-permute-start(bf16[256,256]{1,0:T(8,128)(2,1)} %param.7), channel_id=1, source_target_pairs={{8,0},{12,4},{16,8},{20,12},{24,16},{28,20},{32,24},{36,28},{40,32... | collective-permute-start | bytes 393224 | tf_op jit(solution)/shard_map/ppermute | solution.py:12
  32.9 1.2 collective-permute-done.3
  35.7 41.1 %all-gather.2.cloned.1.call-done = bf16[5,1024,256]{2,1,0:T(8,128)(2,1)} async-done(((bf16[5,256,256]{2,1,0:T(8,128)(2,1)}), bf16[5,1024,256]{2,1,0:T(8,128)(2,1)}) %all-gather.2.cloned.1.call-update) | async-done | bytes 2621456 | tf_op jit(solution)/shard_map/all_gather | solution.py:29
  76.8 4.3 gather_fusion
  81.1 5.6 fusion.20
  86.7 6.7 copy.24
  93.4 4.2 fusion.2
  97.6 1.3 copy.17
  99.2 29.6 %reduce-scatter.3.cloned.1.call-done = f32[256,256]{1,0:T(8,128)} async-done(((f32[1024,256]{1,0:T(8,128)}), f32[256,256]{1,0:T(8,128)}) %reduce-scatter.3.cloned.1.call-update) | async-done | bytes 262160 | tf_op jit(solution)/shard_map/reduce_scatter | solution.py:38
  128.8 1.9 multiply_convert_fusion
  130.9 11.0 %all_gather.7 = bf16[1024,256]{1,0:T(8,128)(2,1)S(1)} all-gather(bf16[256,256]{1,0:T(8,128)(2,1)S(1)} %convolution_convert_fusion), channel_id=1, replica_groups=mesh['dom'=192,'help'=4] {'help'}, dimensions={0}, use_global_device_ids=true | all-gather | bytes 655360 | tf_op jit(solution)/shard_map/all_gather | solution.py:54
  141.9 2.6 gather_fusion.1
  144.5 5.6 fusion.22
  150.1 6.7 copy.25
  156.8 5.1 fusion.18
  162.9 9.1 %collective-permute-start.4 = (bf16[1024,256]{1,0:T(8,128)(2,1)}, bf16[1024,256]{1,0:T(8,128)(2,1)S(1)}, u32[]{:S(2)}, u32[]{:S(2)}) collective-permute-start(bf16[1024,256]{1,0:T(8,128)(2,1)} %bitcast.13), channel_id=1, source_target_pairs={{8,0},{12,4},{16,8},{20,12},{24,16},{28,20},{32,24},{36,28},{40,32... | collective-permute-start | bytes 1572872 | tf_op jit(solution)/shard_map/ppermute | solution.py:12
  172.9 6.2 collective-permute-start.5
  180.0 2.0 collective-permute-start.6
  182.9 1.9 collective-permute-start.7
  185.3 0.9 convolution_bitcast_fusion
  186.2 0.9 fusion.8
  187.2 3.3 collective-permute-done.6
  190.5 14.3 %collective-permute-done.7 = bf16[1024,256]{1,0:T(8,128)(2,1)} collective-permute-done((bf16[1024,256]{1,0:T(8,128)(2,1)}, bf16[1024,256]{1,0:T(8,128)(2,1)}, u32[]{:S(2)}, u32[]{:S(2)}) %collective-permute-start.7) | collective-permute-done | bytes 524320 | tf_op jit(solution)/shard_map/ppermute | solution.py:12
  204.9 2.5 fusion.7
  207.6 443.3 %all-reduce.3.cloned.1.call-done = (f32[256,256]{0,1:T(8,128)}, f32[256,256]{1,0:T(8,128)}) async-done(((f32[256,256]{0,1:T(8,128)}, f32[256,256]{1,0:T(8,128)}), (f32[256,256]{0,1:T(8,128)}, f32[256,256]{1,0:T(8,128)})) %all-reduce.3.cloned.1.call-update) | async-done | bytes 524304 | tf_op jit(solution)/shard_map/psum | solution.py:50
  651.0 1.8 copy.23
  652.7 26.8 %reduce-scatter.5.cloned.1.call-done = bf16[256,256]{1,0:T(8,128)(2,1)} async-done(((bf16[1024,256]{1,0:T(8,128)(2,1)}), bf16[256,256]{1,0:T(8,128)(2,1)}) %reduce-scatter.5.cloned.1.call-update) | async-done | bytes 131088 | tf_op jit(solution)/shard_map/reduce_scatter | solution.py:75
  679.5 1.6 convert_add_fusion
  681.2 1.7 copy.32
  (50 shorter events, 7.5 us)
Async XLA Ops:
  7.2 74.0 %copy-start = (bf16[48,128,128]{2,1,0:T(8,128)(2,1)S(1)}, bf16[48,128,128]{2,1,0:T(8,128)(2,1)}, u32[]{:S(2)}) copy-start(bf16[48,128,128]{2,1,0:T(8,128)(2,1)} %param.8) | copy-start | bytes 4718596
  7.2 69.6 %all-gather.2.cloned.1.call-start = ((), (), s32[]{:S(2)}) async-start(), calls=%async_computation.2 | async-start | bytes 3276800 | tf_op jit(solution)/shard_map/all_gather | solution.py:29
  7.2 24.6 %collective-permute-start = (bf16[256,256]{1,0:T(8,128)(2,1)}, bf16[256,256]{1,0:T(8,128)(2,1)S(1)}, u32[]{:S(2)}, u32[]{:S(2)}) collective-permute-start(bf16[256,256]{1,0:T(8,128)(2,1)} %param.7), channel_id=1, source_target_pairs={{760,0},{764,4},{0,8},{4,12},{8,16},{12,20},{16,24},{20,28},{24,32... | collective-permute-start | bytes 393224 | tf_op jit(solution)/shard_map/ppermute | solution.py:12
  12.2 19.7 %collective-permute-start.1 = (bf16[256,256]{1,0:T(8,128)(2,1)}, bf16[256,256]{1,0:T(8,128)(2,1)S(1)}, u32[]{:S(2)}, u32[]{:S(2)}) collective-permute-start(bf16[256,256]{1,0:T(8,128)(2,1)} %param.7), channel_id=1, source_target_pairs={{764,0},{0,4},{4,8},{8,12},{12,16},{16,20},{20,24},{24,28},{28,32}... | collective-permute-start | bytes 393224 | tf_op jit(solution)/shard_map/ppermute | solution.py:12
  17.0 15.8 %collective-permute-start.2 = (bf16[256,256]{1,0:T(8,128)(2,1)}, bf16[256,256]{1,0:T(8,128)(2,1)S(1)}, u32[]{:S(2)}, u32[]{:S(2)}) collective-permute-start(bf16[256,256]{1,0:T(8,128)(2,1)} %param.7), channel_id=1, source_target_pairs={{4,0},{8,4},{12,8},{16,12},{20,16},{24,20},{28,24},{32,28},{36,32}... | collective-permute-start | bytes 393224 | tf_op jit(solution)/shard_map/ppermute | solution.py:12
  23.7 10.5 %collective-permute-start.3 = (bf16[256,256]{1,0:T(8,128)(2,1)}, bf16[256,256]{1,0:T(8,128)(2,1)S(1)}, u32[]{:S(2)}, u32[]{:S(2)}) collective-permute-start(bf16[256,256]{1,0:T(8,128)(2,1)} %param.7), channel_id=1, source_target_pairs={{8,0},{12,4},{16,8},{20,12},{24,16},{28,20},{32,24},{36,28},{40,32... | collective-permute-start | bytes 393224 | tf_op jit(solution)/shard_map/ppermute | solution.py:12
  34.1 0.8 copy-start.2
  35.0 93.8 %reduce-scatter.3.cloned.1.call-start = ((), (), s32[]{:S(2)}) async-start(), calls=%async_computation.3 | async-start | bytes 1310720 | tf_op jit(solution)/shard_map/reduce_scatter | solution.py:38
  86.7 6.7 copy-start.7
  97.5 1.5 copy-start.1
  97.6 1.5 copy-start.3
  97.6 31.3 %copy-start.5 = (bf16[256,256]{1,0:T(8,128)(2,1)S(1)}, bf16[256,256]{1,0:T(8,128)(2,1)}, u32[]{:S(2)}) copy-start(bf16[256,256]{1,0:T(8,128)(2,1)} %param.12) | copy-start | bytes 393220
  97.6 31.2 %copy-start.8 = (bf16[256,256]{1,0:T(8,128)(2,1)S(1)}, bf16[256,256]{1,0:T(8,128)(2,1)}, u32[]{:S(2)}) copy-start(bf16[256,256]{1,0:T(8,128)(2,1)} %param.13) | copy-start | bytes 393220
  98.9 552.0 %all-reduce.3.cloned.1.call-start = ((), (), s32[]{:S(2)}) async-start(), calls=%async_computation.5 | async-start | bytes 1048576 | tf_op jit(solution)/shard_map/psum | solution.py:50
  150.1 6.7 copy-start.6
  162.9 24.3 %collective-permute-start.4 = (bf16[1024,256]{1,0:T(8,128)(2,1)}, bf16[1024,256]{1,0:T(8,128)(2,1)S(1)}, u32[]{:S(2)}, u32[]{:S(2)}) collective-permute-start(bf16[1024,256]{1,0:T(8,128)(2,1)} %bitcast.13), channel_id=1, source_target_pairs={{8,0},{12,4},{16,8},{20,12},{24,16},{28,20},{32,24},{36,28},{40,32... | collective-permute-start | bytes 1572872 | tf_op jit(solution)/shard_map/ppermute | solution.py:12
  172.9 14.3 %collective-permute-start.5 = (bf16[1024,256]{1,0:T(8,128)(2,1)}, bf16[1024,256]{1,0:T(8,128)(2,1)}, u32[]{:S(2)}, u32[]{:S(2)}) collective-permute-start(bf16[1024,256]{1,0:T(8,128)(2,1)} %bitcast.14), channel_id=1, source_target_pairs={{4,0},{8,4},{12,8},{16,12},{20,16},{24,20},{28,24},{32,28},{36,32}... | collective-permute-start | bytes 1572872 | tf_op jit(solution)/shard_map/ppermute | solution.py:12
  180.0 6.2 copy-start.4
  180.0 10.5 %collective-permute-start.6 = (bf16[1024,256]{1,0:T(8,128)(2,1)}, bf16[1024,256]{1,0:T(8,128)(2,1)}, u32[]{:S(2)}, u32[]{:S(2)}) collective-permute-start(bf16[1024,256]{1,0:T(8,128)(2,1)} %bitcast.15), channel_id=1, source_target_pairs={{764,0},{0,4},{4,8},{8,12},{12,16},{16,20},{20,24},{24,28},{28,32}... | collective-permute-start | bytes 1572872 | tf_op jit(solution)/shard_map/ppermute | solution.py:12
  182.9 21.9 %collective-permute-start.7 = (bf16[1024,256]{1,0:T(8,128)(2,1)}, bf16[1024,256]{1,0:T(8,128)(2,1)}, u32[]{:S(2)}, u32[]{:S(2)}) collective-permute-start(bf16[1024,256]{1,0:T(8,128)(2,1)} %bitcast.16), channel_id=1, source_target_pairs={{760,0},{764,4},{0,8},{4,12},{8,16},{12,20},{16,24},{20,28},{24,32... | collective-permute-start | bytes 1572872 | tf_op jit(solution)/shard_map/ppermute | solution.py:12
  187.2 492.3 %reduce-scatter.5.cloned.1.call-start = ((), (), s32[]{:S(2)}) async-start(), calls=%async_computation.4 | async-start | bytes 655360 | tf_op jit(solution)/shard_map/reduce_scatter | solution.py:75
Sparse Core Ops, SparseCore 0:
  35.1 41.6 all-gather.1
  99.1 29.7 reduce-scatter.2
  187.3 463.6 all-reduce.2
  653.9 25.5 reduce-scatter.4
where the time goes:
time: 691 us; the launch traced here: 689 us
  waiting for transfers between devices  560 us (81%)
  starting transfers between devices  44 us (6%)
  local copies, waits for them, and re-layouts  31 us (4%)
  matrix products  24.8 us (4%)
  between operations  14.1 us (2%)
  blocking collectives  11 us (2%)
    psum x1, waiting for transfers between devices, on_device(): grad_self, grad_neigh = lax.psum((self_term, neigh_term), ('dom', 'help'))  443 us
    ppermute x8, starting transfers between devices, shifted_2(): return lax.ppermute(block, axis, route)  43.9 us
    all_gather x1, waiting for transfers between devices, on_device(): gathered = lax.all_gather(band_local, 'help', axis=1, tiled=True)  41.1 us
    reduce_scatter x1, waiting for transfers between devices, on_device(): lax.psum_scatter(partial_agg, 'help', scatter_dimension=0, tiled=True)  29.6 us
    reduce_scatter x1, waiting for transfers between devices, on_device(): lax.psum_scatter(arrived.astype(jnp.bfloat16), 'help', scatter_dimension=...  26.8 us
    ppermute x8, waiting for transfers between devices, shifted_2(): return lax.ppermute(block, axis, route)  18.9 us
  transfers between devices with their start and end apart: 12, of which 7 were waited for; matrix products, arithmetic and copies ran while one was open for 2% of the time, Pallas kernels for 0%

commit v1 on v0

v1 whole, which is shorter than its diff:
```python
import functools

import jax
import jax.numpy as jnp
from jax import lax
from jax.experimental import pallas as pl
from jax.experimental.pallas import tpu as pltpu
from jax.sharding import PartitionSpec as P

MESH = pl.DeviceIdType.MESH
F32, BF16 = jnp.float32, jnp.bfloat16
HELP = 4
Z_SIZE = 12
UNROLL = 16


def kernel(
    n_dom,
    dst_hbm,
    src_hbm,
    feat_hbm,
    tiles_hbm,
    ws_hbm,
    wn_hbm,
    cot_hbm,
    hid_hbm,
    gf_hbm,
    gw_hbm,
    hid_ref,
    gf_ref,
    gw_ref,
    keys,
    feat_ref,
    ws_ref,
    wn_ref,
    cot_ref,
    tiles,
    order_v,
    idx,
    band,
    prods,
    part,
    relay,
    part_in,
    dest,
    mats,
    mats_out,
    ar_sib,
    ar_x,
    ar_xin,
    ar_z,
    ar_fin,
    sib_out,
    sib_in,
    g,
    za_in,
    rb_in,
    fb_in,
    zb_out,
    zb_in,
    ra_in,
    fa_in,
    own_pre,
    send_sem,
    recv_sem,
    local_sem,
    far_sem,
):
    n_y = n_dom // (2 * Z_SIZE)
    n_tiles, blk = tiles.shape[0], tiles.shape[1]
    half = blk // 2
    d, h = lax.axis_index("dom"), lax.axis_index("help")
    c, k = d % 2, d // 2
    z, y = k % Z_SIZE, k // Z_SIZE
    hr, hl, ho = (h + 1) % HELP, (h + 3) % HELP, (h + 2) % HELP

    sib = (d + 1 - 2 * c, h)
    right, left = (d, hr), (d, hl)

    def xy_peer(i, j):
        return ((((y + j) % n_y) * Z_SIZE + z) * 2 + c, (h + i) % HELP)

    znext, zprev = ((d + 2) % n_dom, h), ((d + n_dom - 2) % n_dom, h)
    y_peers = [xy_peer(0, j) for j in range(1, n_y)]
    def hops(steps, size):
        return min(steps, size - steps)

    xy_steps = [(i, j) for i in range(HELP) for j in range(n_y) if i or j]
    xy_steps.sort(key=lambda ij: -hops(ij[0], HELP) - hops(ij[1], n_y))
    z_steps = sorted(range(1, Z_SIZE), key=lambda j: -hops(j, Z_SIZE))
    z_peers = [((y * Z_SIZE + (z + j) % Z_SIZE) * 2 + c, h) for j in range(1, Z_SIZE)]

    barrier = pltpu.get_barrier_semaphore()
    near = [sib, right, left, znext, zprev, z_peers[0], z_peers[-1], y_peers[0], y_peers[-1]]
    for peer in near:
        pl.semaphore_signal(barrier, inc=1, device_id=peer, device_id_type=MESH)
    local = [
        pltpu.make_async_copy(source, target, local_sem.at[i])
        for i, (source, target) in enumerate(
            (
                (feat_hbm, feat_ref),
                (dst_hbm, keys.at[0]),
                (src_hbm, keys.at[1]),
                (ws_hbm, ws_ref),
                (wn_hbm, wn_ref),
                (cot_hbm, cot_ref),
                (tiles_hbm, tiles),
            )
        )
    ]
    for copy in local:
        copy.start()
    pl.semaphore_wait(barrier, len(near))

    def farther(ring, first):
        for i, peer in enumerate((ring[0], ring[-1])):
            pl.semaphore_signal(
                far_sem.at[first + i], inc=1, device_id=peer, device_id_type=MESH
            )

        def heard():
            for i in range(2):
                pl.semaphore_wait(far_sem.at[first + i], 1)

        return heard

    rounds = [(z_peers, 0)] * (Z_SIZE // 2 - 1) + [(y_peers, 2)] * (n_y // 2 - 1)
    rounds = [rounds[i] for i in sorted(range(len(rounds)), key=lambda i: rounds[:i].count(rounds[i]))]
    waiting = {}

    def next_round():
        if rounds:
            ring, first = rounds.pop(0)
            if first in waiting:
                waiting.pop(first)()
            waiting[first] = farther(ring, first)

    names, started = {}, []

    def send(name, src, dst, device):
        i = names.setdefault(name, len(names))
        copy = pltpu.make_async_remote_copy(
            src_ref=src,
            dst_ref=dst,
            send_sem=send_sem.at[i],
            recv_sem=recv_sem.at[i],
            device_id=device,
            device_id_type=MESH,
        )
        copy.start()
        started.append(copy)

    def arrive(name, dst):
        i = names[name]
        pltpu.make_async_remote_copy(
            src_ref=dst,
            dst_ref=dst,
            send_sem=send_sem.at[i],
            recv_sem=recv_sem.at[i],
            device_id=sib,
            device_id_type=MESH,
        ).wait_recv()

    lo, hi = pl.ds(0, half), pl.ds(half, half)
    q0 = c + 2
    q1 = 4 - 3 * c
    qs = (c, c + 4)

    def at(q, helper, a):
        return band.at[q * 8 + helper * 2 + a]

    def pair(q, helper):
        return band.at[pl.ds(q * 8 + helper * 2, 2)]

    fa, fb = feat_hbm.at[0], feat_hbm.at[1]
    send("a_r", fa, at(q0, h, 0), right)
    send("a_l", fa, at(q0, h, 0), left)
    send("b_n", fb, at(qs[0], h, 1), znext)
    send("b_p", fb, at(qs[1], h, 1), zprev)
    send("b_r", fb, at(q0, h, 1), right)
    send("b_l", fb, at(q0, h, 1), left)
    send("a_n", fa, at(qs[0], h, 0), znext)
    send("a_p", fa, at(qs[1], h, 0), zprev)
    send("s_own", feat_hbm, pair(q0, h), sib)
    next_round()
    next_round()
    local[0].wait()
    band[q0 * 8 + h * 2] = feat_ref[0]
    band[q0 * 8 + h * 2 + 1] = feat_ref[1]
    for copy in local[1:3]:
        copy.wait()
    write_order(keys, order_v, n_tiles)
    order = pltpu.make_async_copy(order_v, idx, local_sem.at[7])
    order.start()

    arrive("a_r", at(q0, hl, 0))
    send("a_rr", at(q0, hl, 0).at[lo], at(q0, hl, 0).at[lo], right)
    send("al_n", at(q0, hl, 0), at(qs[0], hl, 0), znext)
    send("al_p", at(q0, hl, 0), at(qs[1], hl, 0), zprev)
    arrive("a_l", at(q0, hr, 0))
    send("a_ll", at(q0, hr, 0).at[hi], at(q0, hr, 0).at[hi], left)
    send("ar_n", at(q0, hr, 0), at(qs[0], hr, 0), znext)
    send("ar_p", at(q0, hr, 0), at(qs[1], hr, 0), zprev)
    arrive("b_n", at(qs[0], h, 1))
    send("bn_r", at(qs[0], h, 1), at(qs[0], h, 1), right)
    send("bn_l", at(qs[0], h, 1), at(qs[0], h, 1), left)
    arrive("b_p", at(qs[1], h, 1))
    send("bp_r", at(qs[1], h, 1), at(qs[1], h, 1), right)
    send("bp_l", at(qs[1], h, 1), at(qs[1], h, 1), left)
    arrive("b_r", at(q0, hl, 1))
    send("b_rr", at(q0, hl, 1).at[lo], at(q0, hl, 1).at[lo], right)
    send("s_l", pair(q0, hl), pair(q0, hl), sib)
    arrive("b_l", at(q0, hr, 1))
    send("b_ll", at(q0, hr, 1).at[hi], at(q0, hr, 1).at[hi], left)
    send("s_r", pair(q0, hr), pair(q0, hr), sib)
    arrive("a_rr", at(q0, ho, 0).at[lo])
    arrive("a_ll", at(q0, ho, 0).at[hi])
    send("ao_n", at(q0, ho, 0), at(qs[0], ho, 0), znext)
    send("ao_p", at(q0, ho, 0), at(qs[1], ho, 0), zprev)
    arrive("bn_r", at(qs[0], hl, 1))
    send("bn_rr", at(qs[0], hl, 1).at[lo], at(qs[0], hl, 1).at[lo], right)
    arrive("bn_l", at(qs[0], hr, 1))
    send("bn_ll", at(qs[0], hr, 1).at[hi], at(qs[0], hr, 1).at[hi], left)
    arrive("bp_r", at(qs[1], hl, 1))
    send("bp_rr", at(qs[1], hl, 1).at[lo], at(qs[1], hl, 1).at[lo], right)
    next_round()
    next_round()
    arrive("bp_l", at(qs[1], hr, 1))
    send("bp_ll", at(qs[1], hr, 1).at[hi], at(qs[1], hr, 1).at[hi], left)
    arrive("a_n", at(qs[0], h, 0))
    arrive("a_p", at(qs[1], h, 0))
    send("t_own", pair(q1, h), pair(q1, h), sib)
    for copy in local[3:]:
        copy.wait()
    order.wait()
    rows, width = 2 * blk, feat_ref.shape[2]
    feats = feat_ref[...].reshape(rows, width)
    own_pre[...] = jnp.dot(feats, ws_ref[...], preferred_element_type=F32)
    arrive("b_rr", at(q0, ho, 1).at[lo])
    arrive("b_ll", at(q0, ho, 1).at[hi])
    send("s_o", pair(q0, ho), pair(q0, ho), sib)
    arrive("al_n", at(qs[0], hl, 0))
    arrive("al_p", at(qs[1], hl, 0))
    send("t_l", pair(q1, hl), pair(q1, hl), sib)
    arrive("ar_n", at(qs[0], hr, 0))
    arrive("ar_p", at(qs[1], hr, 0))
    send("t_r", pair(q1, hr), pair(q1, hr), sib)
    arrive("bn_rr", at(qs[0], ho, 1).at[lo])
    arrive("bn_ll", at(qs[0], ho, 1).at[hi])
    arrive("bp_rr", at(qs[1], ho, 1).at[lo])
    arrive("bp_ll", at(qs[1], ho, 1).at[hi])
    next_round()
    next_round()
    arrive("ao_n", at(qs[0], ho, 0))
    arrive("ao_p", at(qs[1], ho, 0))
    send("t_o", pair(q1, ho), pair(q1, ho), sib)
    p0, p1 = 3 - c, 1 + 3 * c
    for name, q, helper in (
        ("s_own", p0, h),
        ("s_l", p0, hl),
        ("s_r", p0, hr),
        ("t_own", p1, h),
        ("s_o", p0, ho),
        ("t_l", p1, hl),
        ("t_r", p1, hr),
        ("t_o", p1, ho),
    ):
        arrive(name, pair(q, helper))

    def forward(step, total):
        for u in range(UNROLL):
            i = step * UNROLL + u
            t = idx[0, i]
            s = idx[1, i] + 8 * c
            product = jnp.dot(tiles[t], band[s], preferred_element_type=F32)
            total = product + jnp.where(idx[2, i] > 0, total, 0.0)
            prods[i] = total.astype(BF16)
        return total

    zero = jnp.zeros((blk, band.shape[2]), F32)
    lax.fori_loop(0, n_tiles // UNROLL, forward, zero)

    def block_of(way, b):
        return jnp.where(idx[way + 4, b] > 0, prods[idx[way + 3, b]], jnp.zeros((), BF16))

    def owner_blocks(helper):
        for a in range(2):
            part[helper * 2 + a] = block_of(0, helper * 2 + a)

    waiting.pop(2)()
    next_round()
    owner_blocks(ho)
    send("p_rr", part.at[ho * 2], relay.at[0], right)
    send("p_ll", part.at[ho * 2 + 1], relay.at[1], left)
    owner_blocks(hr)
    send("p_r1", part.at[hr * 2 + 1], part_in.at[0, 1], right)
    owner_blocks(hl)
    send("p_l0", part.at[hl * 2], part_in.at[1, 0], left)
    owner_blocks(h)
    arrive("p_rr", relay.at[0])
    part[hr * 2] = (part[hr * 2].astype(F32) + relay[0].astype(F32)).astype(BF16)
    send("p_r0", part.at[hr * 2], part_in.at[0, 0], right)
    arrive("p_ll", relay.at[1])
    part[hl * 2 + 1] = (part[hl * 2 + 1].astype(F32) + relay[1].astype(F32)).astype(BF16)
    send("p_l1", part.at[hl * 2 + 1], part_in.at[1, 1], left)
    next_round()
    arrive("p_r1", part_in.at[0, 1])
    arrive("p_l0", part_in.at[1, 0])
    arrive("p_r0", part_in.at[0, 0])
    arrive("p_l1", part_in.at[1, 1])
    summed = part[pl.ds(h * 2, 2)].astype(F32) + part_in[0].astype(F32) + part_in[1].astype(F32)
    aggregate = summed.astype(BF16).reshape(rows, width)

    pre = own_pre[...] + jnp.dot(aggregate, wn_ref[...], preferred_element_type=F32)
    squash = jax.nn.sigmoid(pre)
    slope = squash * (1.0 + pre * (1.0 - squash))
    grad_pre = (cot_ref[...].astype(F32) * slope).astype(BF16)
    over_rows = (((0,), (0,)), ((), ()))
    for which in (1 - c, c):
        left_rows = jnp.where(which == 0, feats, aggregate)
        term = lax.dot_general(left_rows, grad_pre, over_rows, preferred_element_type=F32)
        if which is c:
            mats[...] = term
        else:
            mats_out[...] = term.astype(BF16)
            send("w_sib", mats_out, ar_sib, sib)
    dest_grad = lax.dot_general(
        grad_pre, wn_ref[...], (((1,), (1,)), ((), ())), preferred_element_type=F32
    ).astype(BF16)
    dest[pl.ds(h * 2, 2)] = dest_grad.reshape(2, blk, width)

    def dest_at(helper, a):
        return dest.at[helper * 2 + a]

    for a in range(2):
        send(f"d_r{a}", dest_at(h, a), dest_at(h, a), right)
        send(f"d_l{a}", dest_at(h, 1 - a), dest_at(h, 1 - a), left)
    hid_ref[...] = (pre * squash).astype(BF16)
    results = [(hid_ref, hid_hbm), (gf_ref, gf_hbm)]
    results += [(gw_ref.at[which], gw_hbm.at[which]) for which in (c, 1 - c)]
    results = [pltpu.make_async_copy(*pair, local_sem.at[8 + i]) for i, pair in enumerate(results)]
    results[0].start()
    assert not rounds
    for heard in waiting.values():
        heard()
    arrive("w_sib", ar_sib)
    summed = mats[...] + ar_sib[...].astype(F32)
    chunk_rows, chunk_cols = ar_x.shape[2:]
    quarter = summed.shape[0] // HELP
    for i in range(HELP):
        for j in range(n_y):
            r, s = i * quarter + j // 2 * chunk_rows, j % 2 * chunk_cols
            ar_x[i, j] = summed[r : r + chunk_rows, s : s + chunk_cols].astype(BF16)
    for n, (i, j) in enumerate(xy_steps):
        send(f"w_{i}_{j}", ar_x.at[(h + i) % HELP, (y + j) % n_y], ar_xin.at[n], xy_peer(i, j))
    arrive("d_r0", dest_at(hl, 0))
    send("d_rr", dest_at(hl, 0), dest_at(hl, 0), right)
    arrive("d_l0", dest_at(hr, 1))
    send("d_ll", dest_at(hr, 1), dest_at(hr, 1), left)
    gf_ref[...] = lax.dot_general(
        grad_pre, ws_ref[...], (((1,), (1,)), ((), ())), preferred_element_type=F32
    )
    arrive("d_r1", dest_at(hl, 1))
    arrive("d_l1", dest_at(hr, 0))
    arrive("d_rr", dest_at(ho, 0))
    arrive("d_ll", dest_at(ho, 1))

    def backward(step, total):
        for u in range(UNROLL):
            i = step * UNROLL + u
            t = idx[8, i]
            s = idx[9, i]
            product = lax.dot_general(
                tiles[t], dest[s], over_rows, preferred_element_type=F32
            )
            total = product + jnp.where(idx[10, i] > 0, total, 0.0)
            prods[i] = total.astype(BF16)
        return total

    steps = n_tiles // UNROLL
    total = lax.fori_loop(0, steps * 2 // 3, backward, zero)
    for n, (i, j) in reversed(list(enumerate(xy_steps))):
        arrive(f"w_{i}_{j}", ar_xin.at[n])
    chunk = ar_x[h, y].astype(F32) + jnp.sum(ar_xin[...].astype(F32), axis=0)
    ar_z[z] = chunk.astype(BF16)
    for j in z_steps:
        send(f"w_z{j}", ar_z.at[z], ar_z.at[z], z_peers[j - 1])
    lax.fori_loop(steps * 2 // 3, steps, backward, total)

    SOLO, MID, OTH = 0, 1, 2
    base = (32 * c, 16, 32 - 32 * c)
    sib_base = (None, 8 * (3 - 2 * c), 8 * (2 * c + 1))
    to = (((d + n_dom - 2 + 4 * c) % n_dom, h), None, ((d + n_dom + 2 - 4 * c) % n_dom, h))

    def pass_over(kind, a):
        def body(helper, carry):
            sib_out[kind - 1, a, helper] = block_of(8, sib_base[kind] + helper * 2 + a)
            return carry

        lax.fori_loop(0, HELP, body, 0)
        send(f"e_{kind}{a}", sib_out.at[kind - 1, a], sib_in.at[kind - 1, a], sib)

    def take(kind, a):
        if kind != SOLO:
            arrive(f"e_{kind}{a}", sib_in.at[kind - 1, a])

        def body(helper, carry):
            mine = block_of(8, base[kind] + helper * 2 + a)
            if kind != SOLO:
                mine = (mine.astype(F32) + sib_in[kind - 1, a, helper].astype(F32)).astype(BF16)
            g[kind, a, helper] = mine
            return carry

        lax.fori_loop(0, HELP, body, 0)
        if a == 1:
            send(f"rb_r{kind}", g.at[kind, 1, ho].at[lo], rb_in.at[0, kind], right)
            send(f"rb_l{kind}", g.at[kind, 1, ho].at[hi], rb_in.at[1, kind], left)
        elif kind != MID:
            for i, helper in enumerate((ho, hr, hl, h)):
                send(f"za_{kind}{i}", g.at[kind, 0, helper], za_in.at[kind // 2, i], to[kind])

    def pass_on(kind):
        arrive(f"rb_r{kind}", rb_in.at[0, kind])
        g[kind, 1, hr, lo] = (g[kind, 1, hr, lo].astype(F32) + rb_in[0, kind].astype(F32)).astype(BF16)
        send(f"fb_r{kind}", g.at[kind, 1, hr], fb_in.at[0, kind], right)
        arrive(f"rb_l{kind}", rb_in.at[1, kind])
        g[kind, 1, hl, hi] = (g[kind, 1, hl, hi].astype(F32) + rb_in[1, kind].astype(F32)).astype(BF16)
        send(f"fb_l{kind}", g.at[kind, 1, hl], fb_in.at[1, kind], left)

    def finish(kind):
        arrive(f"fb_r{kind}", fb_in.at[0, kind])
        arrive(f"fb_l{kind}", fb_in.at[1, kind])
        total = g[kind, 1, h].astype(F32) + fb_in[0, kind].astype(F32) + fb_in[1, kind].astype(F32)
        if kind == MID:
            gf_ref[pl.ds(blk, blk)] += total
        else:
            zb_out[kind // 2] = total.astype(BF16)
            send(f"zb_{kind}", zb_out.at[kind // 2], zb_in.at[kind // 2], to[kind])

    def add_z(i, helper):
        arrive(f"za_{SOLO}{i}", za_in.at[0, i])
        arrive(f"za_{OTH}{i}", za_in.at[1, i])
        total = g[MID, 0, helper].astype(F32) + za_in[0, i].astype(F32) + za_in[1, i].astype(F32)
        g[MID, 0, helper] = total.astype(BF16)

    pass_over(OTH, 1)
    pass_over(OTH, 0)
    take(SOLO, 1)
    take(SOLO, 0)
    pass_over(MID, 1)
    pass_over(MID, 0)
    take(OTH, 1)
    take(OTH, 0)
    take(MID, 1)
    pass_on(SOLO)
    take(MID, 0)
    for j in z_steps[::-1]:
        arrive(f"w_z{j}", ar_z.at[(z + Z_SIZE - j) % Z_SIZE])
    chunk = ar_z[0].astype(F32)
    for j in range(1, Z_SIZE):
        chunk = chunk + ar_z[j].astype(F32)
    ar_fin[c, h, y] = chunk.astype(BF16)
    for i, j in xy_steps:
        send(f"v_{i}_{j}", ar_fin.at[c, h, y], ar_fin.at[c, h, y], xy_peer(i, j))
    pass_on(OTH)
    pass_on(MID)
    finish(SOLO)
    add_z(0, ho)
    send("ra_r", g.at[MID, 0, ho].at[lo], ra_in.at[0], right)
    send("ra_l", g.at[MID, 0, ho].at[hi], ra_in.at[1], left)
    add_z(1, hr)
    add_z(2, hl)
    add_z(3, h)
    finish(OTH)
    arrive("ra_r", ra_in.at[0])
    g[MID, 0, hr, lo] = (g[MID, 0, hr, lo].astype(F32) + ra_in[0].astype(F32)).astype(BF16)
    send("fa_r", g.at[MID, 0, hr], fa_in.at[0], right)
    arrive("ra_l", ra_in.at[1])
    g[MID, 0, hl, hi] = (g[MID, 0, hl, hi].astype(F32) + ra_in[1].astype(F32)).astype(BF16)
    send("fa_l", g.at[MID, 0, hl], fa_in.at[1], left)

    finish(MID)
    for kind in (SOLO, OTH):
        arrive(f"zb_{kind}", zb_in.at[kind // 2])
        gf_ref[pl.ds(blk, blk)] += zb_in[kind // 2].astype(F32)
    arrive("fa_r", fa_in.at[0])
    arrive("fa_l", fa_in.at[1])
    gf_ref[pl.ds(0, blk)] += (
        g[MID, 0, h].astype(F32) + fa_in[0].astype(F32) + fa_in[1].astype(F32)
    )
    results[1].start()
    def write(which):
        for helper in range(HELP):
            for j in range(n_y):
                r, s = helper * quarter + j // 2 * chunk_rows, j % 2 * chunk_cols
                gw_ref[which, r : r + chunk_rows, s : s + chunk_cols] = ar_fin[
                    which, helper, j
                ].astype(F32)

    def all_sent():
        while started:
            started.pop(0).wait_send()

    all_sent()
    for i in (0, 1, 3, 2):
        helper = (h + HELP - i) % HELP
        for j in range(n_y):
            if i or j:
                arrive(f"v_{i}_{j}", ar_fin.at[c, helper, (y + n_y - j) % n_y])
        send(f"v_s{i}", ar_fin.at[c, helper], ar_fin.at[c, helper], sib)
    write(c)
    results[2].start()
    for i in range(HELP):
        arrive(f"v_s{i}", ar_fin.at[1 - c, (h + HELP - i) % HELP])
    write(1 - c)
    results[3].start()
    all_sent()
    for result in results:
        result.wait()
    assert len(names) == send_sem.shape[0]


def write_order(keys, order_v, n_tiles):
    shape = (n_tiles, order_v.shape[1])
    at = lax.broadcasted_iota(jnp.int32, shape, 0)
    lane = lax.broadcasted_iota(jnp.int32, shape, 1)
    tile = lane < n_tiles

    def column(row):
        return jnp.sum(jnp.where(at == lane, row, 0), axis=1, keepdims=True)

    rows = [jnp.broadcast_to(keys[i], (n_tiles, n_tiles)) for i in range(2)]
    pad = jnp.zeros((n_tiles, shape[1] - n_tiles), jnp.int32)
    rows = [jnp.concatenate([row, pad], axis=1) for row in rows]
    columns = [column(row) for row in rows]
    for way in range(2):
        row, key, other = rows[way], columns[way], columns[1 - way]
        tied = tile & (row == key) & (lane < at)
        before = tile & (row < key)
        rank = jnp.sum(jnp.where(tied | before, 1, 0), axis=1, keepdims=True)
        again = jnp.max(jnp.where(tied, 1, 0), axis=1, keepdims=True)
        here = rank == lane

        def total(values):
            return jnp.sum(values, axis=0, keepdims=True)

        results = (
            total(jnp.where(here, at, 0)),
            total(jnp.where(here, other, 0)),
            total(jnp.where(here, again, 0)),
            jnp.maximum(total(jnp.where(key <= lane, 1, 0)) - 1, 0),
            total(jnp.where(key == lane, 1, 0)),
        )
        for i, result in enumerate(results):
            order_v[pl.ds(way * 8 + i, 1), :] = result


def hand_over(*refs):
    sources, outs, held, sem = refs[:3], refs[3:7], refs[7:11], refs[11]
    sources = (*sources[:2], sources[2].at[0], sources[2].at[1])
    arrivals = [
        pltpu.make_async_copy(source, to, sem.at[i])
        for i, (source, to) in enumerate(zip(sources, held))
    ]
    leaving = [
        pltpu.make_async_copy(to, out, sem.at[4 + i])
        for i, (to, out) in enumerate(zip(held, outs))
    ]
    for copy in arrivals:
        copy.start()
    for arrival, copy in zip(arrivals, leaving):
        arrival.wait()
        copy.start()
    for copy in leaving:
        copy.wait()


def on_device(features, tile_vals, tile_dst, tile_src, w_self, w_neigh, cotangent):
    n_dom = lax.axis_size("dom")
    n_y = n_dom // (2 * Z_SIZE)
    rows, width = features.shape
    n_tiles, blk = tile_vals.shape[:2]
    quarter = width // HELP
    chunk = (n_y, quarter * 2 // n_y, width // 2)
    copies = 34 + 6 + 6 + 4 + 26 + 1 + HELP + 2 * (HELP * n_y - 1) + (Z_SIZE - 1)
    V = lambda *shape: pltpu.VMEM(shape, BF16)
    hbm = pl.BlockSpec(memory_space=pl.ANY)
    hidden, grad_features, grads = pl.pallas_call(
        functools.partial(kernel, n_dom),
        out_shape=(
            jax.ShapeDtypeStruct((rows, width), BF16),
            jax.ShapeDtypeStruct((rows, width), F32),
            jax.ShapeDtypeStruct((2, width, width), F32),
        ),
        in_specs=[hbm] * 7,
        out_specs=(hbm, hbm, hbm),
        scratch_shapes=[
            V(rows, width),
            pltpu.VMEM((rows, width), F32),
            pltpu.VMEM((2, width, width), F32),
            pltpu.VMEM((2, 1, n_tiles), jnp.int32),
            V(2, blk, width),
            V(width, width),
            V(width, width),
            V(rows, width),
            V(n_tiles, blk, blk),
            pltpu.VMEM((16, 128), jnp.int32),
            pltpu.SMEM((16, 128), jnp.int32),
            V(48, blk, width),
            V(n_tiles, blk, width),
            V(8, blk, width),
            V(2, blk, width),
            V(2, 2, blk, width),
            V(8, blk, width),
            pltpu.VMEM((width, width), F32),
            V(width, width),
            V(width, width),
            V(HELP, *chunk),
            V(HELP * n_y - 1, *chunk[1:]),
            V(Z_SIZE, *chunk[1:]),
            V(2, HELP, *chunk),
            V(2, 2, HELP, blk, width),
            V(2, 2, HELP, blk, width),
            V(3, 2, HELP, blk, width),
            V(2, 4, blk, width),
            V(2, 3, blk // 2, width),
            V(2, 3, blk, width),
            V(2, blk, width),
            V(2, blk, width),
            V(2, blk // 2, width),
            V(2, blk, width),
            pltpu.VMEM((rows, width), F32),
            pltpu.SemaphoreType.DMA((copies,)),
            pltpu.SemaphoreType.DMA((copies,)),
            pltpu.SemaphoreType.DMA((12,)),
            pltpu.SemaphoreType.REGULAR((4,)),
        ],
        compiler_params=pltpu.CompilerParams(
            collective_id=0, has_side_effects=True, vmem_limit_bytes=56 * 1024 * 1024
        ),
    )(
        tile_dst.reshape(1, n_tiles),
        tile_src.reshape(1, n_tiles),
        features.reshape(2, blk, width),
        tile_vals,
        w_self,
        w_neigh,
        cotangent,
    )
    shapes = (((rows, width), BF16), ((rows, width), F32), ((width, width), F32), ((width, width), F32))
    return pl.pallas_call(
        hand_over,
        out_shape=tuple(jax.ShapeDtypeStruct(*shape) for shape in shapes),
        in_specs=[hbm] * 3,
        out_specs=(hbm,) * 4,
        scratch_shapes=[
            *(pltpu.VMEM(*shape) for shape in shapes),
            pltpu.SemaphoreType.DMA((8,)),
        ],
    )(hidden, grad_features, grads)


def solution(mesh):
    in_specs = (
        P(("dom", "help"), None),
        P(("dom", "help"), None, None),
        P(("dom", "help")),
        P(("dom", "help")),
        P(),
        P(),
        P(("dom", "help"), None),
    )
    out_specs = (P(("dom", "help"), None), P(("dom", "help"), None), P(), P())
    return jax.shard_map(
        on_device, mesh=mesh, in_specs=in_specs, out_specs=out_specs, check_vma=False
    )
```

time: 691 us -> 74.5 us (0.11)
  waiting for transfers between devices: 560 us -> 0 us
  Pallas kernels: 0 us -> 73.7 us
  starting transfers between devices: 44 us -> 0 us
  local copies, waits for them, and re-layouts: 31 us -> 0 us
  matrix products: 24.8 us -> 0 us
  between operations: 14.1 us -> 0.64 us
  blocking collectives: 11 us -> 0 us
    psum x1 -> x0, waiting for transfers between devices: 443 us -> none  [on_device(): grad_self, grad_neigh = lax.psum((self_term, neigh_term), ('dom', 'help'))]
    pallas_call x0 -> x2, Pallas kernels: none -> 73.7 us  [the longest x1 71.8 us: on_device(): pl.pallas_call(functools.partial(kernel, n_dom), out_shape=(jax.ShapeDtyp...]
    reduce_scatter x2 -> x0, waiting for transfers between devices: 56.4 us -> none  [the longest x1 29.6 us: on_device(): lax.psum_scatter(partial_agg, 'help', scatter_dimension=0, tiled=True)]
    ppermute x8 -> x0, starting transfers between devices: 43.9 us -> none  [shifted_2(): return lax.ppermute(block, axis, route)]
    all_gather x1 -> x0, waiting for transfers between devices: 41.1 us -> none  [on_device(): gathered = lax.all_gather(band_local, 'help', axis=1, tiled=True)]
    dot_general x10 -> x0, matrix products: 24.8 us -> none  [the longest x1 5.58 us: on_device(): jnp.einsum('tij,tjf->tif', tile_vals, picked, preferred_element_type=jnp....]
    ppermute x8 -> x0, waiting for transfers between devices: 18.9 us -> none  [shifted_2(): return lax.ppermute(block, axis, route)]
    dot_general x3 -> x0, local copies, waits for them, and re-layouts: 14.7 us -> none  [the longest x1 6.67 us: on_device(): jnp.einsum('tij,tjf->tif', tile_vals, picked, preferred_element_type=jnp....]
  transfers between devices with their start and end apart: 12 -> 0, of which waited for: 7 -> 0; matrix products, arithmetic and copies ran while one was open for 2% -> 0% of each run, Pallas kernels for 0% -> 0%
where the time goes in v1:
time: 74.5 us; the launch traced here: 74.4 us
  Pallas kernels  73.7 us (99%)
    pallas_call x1, Pallas kernels, on_device(): pl.pallas_call(functools.partial(kernel, n_dom), out_shape=(jax.ShapeDtyp...  71.8 us
    pallas_call x1, Pallas kernels, on_device(): pl.pallas_call(hand_over, out_shape=tuple((jax.ShapeDtypeStruct(*shape) f...  1.97 us

profile of v1, /device:TPU:1, one launch (start us, length us, event | category | flops | bytes accessed | tf_op | source)
XLA Modules:
  0.0 74.4 jit_solution(15629652611490111655)
XLA Ops:
  0.6 71.8 %shard_map.102 = (bf16[256,256]{1,0:T(8,128)(2,1)}, f32[256,256]{1,0:T(8,128)}, f32[2,256,256]{2,1,0:T(8,128)}) custom-call(s32[1,48]{1,0:T(1,128)} %bitcast.4, s32[1,48]{1,0:T(1,128)} %bitcast.5, bf16[2,128,256]{2,1,0:T(8,128)(2,1)} %bitcast.3, bf16[48,128,128]{2,1,0:T(8,128)(2,1)} %tiles_hbm.1, bf16[256,256]{1,0:T(8,128)(2,1)} %ws_hbm.1, ...), custom_call_target="tpu_custom_call" | custom-call | tf_op jit(solution)/shard_map/pallas_call | solution.py:588
  72.4 2.0 %shard_map.103 = (bf16[256,256]{1,0:T(8,128)(2,1)}, f32[256,256]{1,0:T(8,128)}, f32[256,256]{1,0:T(8,128)}, f32[256,256]{1,0:T(8,128)}) custom-call(bf16[256,256]{1,0:T(8,128)(2,1)} %get-tuple-element.7.refs_0_, f32[256,256]{1,0:T(8,128)} %get-tuple-element.8.refs_1_, f32[2,256,256]{2,1,0:T(8,128)} %get-tuple-element.9.refs_2_), custom_call_target="tpu_custom_call" | custom-call | tf_op jit(solution)/shard_map/pallas_call | solution.py:651

commit v2 on v1

--- a/solution.py
+++ b/solution.py
@@ -11,7 +11,7 @@
 F32, BF16 = jnp.float32, jnp.bfloat16
 HELP = 4
 Z_SIZE = 12
-UNROLL = 16
+FORWARD_UNROLL, UNROLL = 24, 16
 
 
 def kernel(
@@ -268,8 +268,8 @@
         arrive(name, pair(q, helper))
 
     def forward(step, total):
-        for u in range(UNROLL):
-            i = step * UNROLL + u
+        for u in range(FORWARD_UNROLL):
+            i = step * FORWARD_UNROLL + u
             t = idx[0, i]
             s = idx[1, i] + 8 * c
             product = jnp.dot(tiles[t], band[s], preferred_element_type=F32)
@@ -278,7 +278,7 @@
         return total
 
     zero = jnp.zeros((blk, band.shape[2]), F32)
-    lax.fori_loop(0, n_tiles // UNROLL, forward, zero)
+    lax.fori_loop(0, n_tiles // FORWARD_UNROLL, forward, zero)
 
     def block_of(way, b):
         return jnp.where(idx[way + 4, b] > 0, prods[idx[way + 3, b]], jnp.zeros((), BF16))

time: 74.5 us -> 75.1 us (level)
  no operation moved by 1% of the time
where the time goes in v2:
time: 75.1 us; the launch traced here: 74.9 us
  Pallas kernels  74.3 us (99%)
    pallas_call x1, Pallas kernels, on_device(): pl.pallas_call(functools.partial(kernel, n_dom), out_shape=(jax.ShapeDtyp...  72.3 us
    pallas_call x1, Pallas kernels, on_device(): pl.pallas_call(hand_over, out_shape=tuple((jax.ShapeDtypeStruct(*shape) f...  1.97 us

profile of v2, /device:TPU:1, one launch (start us, length us, event | category | flops | bytes accessed | tf_op | source)
XLA Modules:
  0.0 74.9 jit_solution(6276537074198561729)
XLA Ops:
  0.6 72.3 %shard_map.102 = (bf16[256,256]{1,0:T(8,128)(2,1)}, f32[256,256]{1,0:T(8,128)}, f32[2,256,256]{2,1,0:T(8,128)}) custom-call(s32[1,48]{1,0:T(1,128)} %bitcast.4, s32[1,48]{1,0:T(1,128)} %bitcast.5, bf16[2,128,256]{2,1,0:T(8,128)(2,1)} %bitcast.3, bf16[48,128,128]{2,1,0:T(8,128)(2,1)} %tiles_hbm.1, bf16[256,256]{1,0:T(8,128)(2,1)} %ws_hbm.1, ...), custom_call_target="tpu_custom_call" | custom-call | tf_op jit(solution)/shard_map/pallas_call | solution.py:588
  73.0 2.0 %shard_map.103 = (bf16[256,256]{1,0:T(8,128)(2,1)}, f32[256,256]{1,0:T(8,128)}, f32[256,256]{1,0:T(8,128)}, f32[256,256]{1,0:T(8,128)}) custom-call(bf16[256,256]{1,0:T(8,128)(2,1)} %get-tuple-element.7.refs_0_, f32[256,256]{1,0:T(8,128)} %get-tuple-element.8.refs_1_, f32[2,256,256]{2,1,0:T(8,128)} %get-tuple-element.9.refs_2_), custom_call_target="tpu_custom_call" | custom-call | tf_op jit(solution)/shard_map/pallas_call | solution.py:651
